TPU v7x, 32 devices: a whole 2x2x4 slice. The times are simulated.
32 devices in a mesh: groups: 2 (over y), ctx: 4 (over x, core), tp: 4 (over z).
Axes of the slice: x: 2, y: 2, z: 4, core: 2. Of those that a mesh axis runs over, the one named last changes fastest.
Arguments:
- tokens: bfloat16 [2048, 4096], P(('groups', 'ctx', 'tp')), parts along dimension 0, may hold values from -6 to 6
- gate_weight: bfloat16 [4096, 8192], P(None, 'tp'), may hold values from -0.09375 to 0.09375
- value_weight: bfloat16 [4096, 8192], P(None, 'tp'), may hold values from -0.09375 to 0.09375
- key_weight: bfloat16 [4096, 1024], P(None, 'tp'), may hold values from -0.09375 to 0.09375
- query_weight: bfloat16 [4096, 1024], P(None, 'tp'), may hold values from -0.09375 to 0.09375
- step_weight: bfloat16 [4096, 128], P(None, 'tp'), may hold values from -0.09375 to 0.09375
- value_conv: float32 [4, 8192], P(None, 'tp'), may hold values from -3 to 3
- key_conv: float32 [4, 1024], P(None, 'tp'), may hold values from -3 to 3
- query_conv: float32 [4, 1024], P(None, 'tp'), may hold values from -3 to 3
- step_bias: float32 [128], P('tp'), may hold values from -3 to -1
- decay_log: float32 [128], P('tp'), may hold values from -6.5 to -1.5
- skip_gain: float32 [128], P('tp'), may hold values from 0.5 to 1.5
- norm_gain: float32 [8192], P('tp'), may hold values from 0.1 to 1.9
- out_weight: bfloat16 [8192, 4096], P('tp'), may hold values from -0.0625 to 0.0625
Outputs:
- layer_out: bfloat16 [2048, 4096], P(('groups', 'ctx', 'tp')), parts along dimension 0
There are 2 independent parts, one for each index of `groups`. A program takes and returns all parts, laid end to end along the dimension named above; an argument that names none is the same for every part. Nothing has to cross between parts.
All inputs are finite; a program needn't handle non-finite values.
Results may differ from a plain program's by a relative error of at most 0.024.
Values may be sent and summed in bfloat16 or wider, within the bound.
A program may use at most 192 MiB of HBM per device.

v0:
```python
import jax
import jax.numpy as jnp
from jax import lax
from jax.sharding import PartitionSpec as P

STATE = 128
GROUPS = 8
INNER = 8192


def passed_along(shard, axis, by):
    count = lax.axis_size(axis)
    pairs = [(i, i + by) for i in range(count) if 0 <= i + by < count]
    return lax.ppermute(shard, axis, pairs)


def from_partner(block, axis, distance):
    count = lax.axis_size(axis)
    route = []
    for low in range(count):
        high = low | 1 << distance
        if high != low and high < count:
            route += [(low, high), (high, low)]
    return lax.ppermute(block, axis, route)


def causal_mix(padded, kernel, length):
    total = padded[0:length] * kernel[0]
    for tap_index in range(1, kernel.shape[0]):
        total = total + padded[tap_index : tap_index + length] * kernel[tap_index]
    return total


def shards(
    tokens,
    gate_weight,
    value_weight,
    key_weight,
    query_weight,
    step_weight,
    value_conv,
    key_conv,
    query_conv,
    step_bias,
    decay_log,
    skip_gain,
    norm_gain,
    out_weight,
):
    tok_dev = tokens.shape[0]
    slab_rows = tok_dev * lax.axis_size("tp")
    columns = gate_weight.shape[1]
    key_cols = key_weight.shape[1]
    heads_here = step_weight.shape[1]
    head_width = columns // heads_here
    block_len = min(128, slab_rows)
    block_count = slab_rows // block_len
    kernel_len = value_conv.shape[0]
    joined = jnp.concatenate(
        [gate_weight, value_weight, key_weight, query_weight, step_weight], axis=1
    )
    projected = jnp.dot(
        lax.all_gather(tokens, "tp", axis=0, tiled=True), joined, preferred_element_type=jnp.float32
    )
    gate_in = projected[:, :columns].astype(jnp.bfloat16)
    mixed_pre = projected[:, columns : 2 * columns + 2 * key_cols].astype(jnp.bfloat16)
    step_raw = projected[:, 2 * columns + 2 * key_cols :]
    border = passed_along(mixed_pre[slab_rows - (kernel_len - 1) :], "ctx", 1)
    padded = jnp.concatenate([border, mixed_pre], axis=0).astype(jnp.float32)
    kernel = jnp.concatenate([value_conv, key_conv, query_conv], axis=1)
    activated = jax.nn.silu(causal_mix(padded, kernel, slab_rows)).astype(jnp.bfloat16)
    value_act = activated[:, :columns]
    key_act = activated[:, columns : columns + key_cols]
    query_act = activated[:, columns + key_cols :]
    group_cols = max(key_cols, STATE)
    reach = group_cols // key_cols
    key_group, query_group = (key_act, query_act)
    for bit_index in range(reach.bit_length() - 1):
        other_keys, other_queries = from_partner((key_group, query_group), "tp", bit_index)
        upper = lax.axis_index("tp") // (1 << bit_index) % 2 == 1
        key_group = jnp.where(
            upper,
            jnp.concatenate([other_keys, key_group], 1),
            jnp.concatenate([key_group, other_keys], 1),
        )
        query_group = jnp.where(
            upper,
            jnp.concatenate([other_queries, query_group], 1),
            jnp.concatenate([query_group, other_queries], 1),
        )
    local_groups = group_cols // STATE
    per_group = heads_here // local_groups
    step = jax.nn.softplus(step_raw + step_bias)
    rate = -jnp.exp(decay_log) * step
    cum = jnp.cumsum(rate.reshape(block_count, block_len, heads_here), axis=1)
    step_blk = step.reshape(block_count, block_len, heads_here)
    values = value_act.reshape(block_count, block_len, heads_here, head_width)
    keys = key_group.reshape(block_count, block_len, local_groups, STATE)
    queries = query_group.reshape(block_count, block_len, local_groups, STATE)
    scores = jnp.einsum("btgn,bugn->gbtu", queries, keys, preferred_element_type=jnp.float32)
    scores = jnp.repeat(scores, per_group, axis=0)
    cum_t = jnp.transpose(cum, (2, 0, 1))
    step_t = jnp.transpose(step_blk, (2, 0, 1))
    causal = jnp.tril(jnp.ones((block_len, block_len), jnp.bool_))
    diff = cum_t[:, :, :, None] - cum_t[:, :, None, :]
    factor = jnp.where(causal, jnp.exp(jnp.where(causal, diff, 0.0)), 0.0)
    weights = (scores * factor * step_t[:, :, None, :]).astype(jnp.bfloat16)
    inner = jnp.einsum("hbtu,buhp->bthp", weights, values, preferred_element_type=jnp.float32)
    tail = jnp.exp(cum[:, -1:, :] - cum) * step_blk
    weighted = (values * tail[:, :, :, None]).astype(jnp.bfloat16)
    key_heads = jnp.repeat(keys, per_group, axis=2)
    query_heads = jnp.repeat(queries, per_group, axis=2)
    local = jnp.einsum("buhn,buhp->bhnp", key_heads, weighted, preferred_element_type=jnp.float32)
    falloff = jnp.exp(cum[:, -1, :])

    def advance(carry, item):
        fade, added = item
        return (fade[:, None, None] * carry + added, carry)

    zero_state = jnp.zeros((heads_here, STATE, head_width), jnp.float32)
    slab_state, _ = lax.scan(advance, zero_state, (falloff, local))
    slab_fall = jnp.exp(jnp.sum(cum[:, -1, :], axis=0))
    inflow = zero_state
    for turn in range(lax.axis_size("ctx") - 1):
        inflow = passed_along(
            (slab_fall[:, None, None] * inflow + slab_state).astype(jnp.bfloat16), "ctx", 1
        ).astype(jnp.float32)
    _, starts = lax.scan(advance, inflow, (falloff, local))
    outer = jnp.einsum(
        "bthn,bhnp->bthp", query_heads.astype(jnp.float32), starts, precision=lax.Precision.HIGHEST
    )
    ssm_out = (
        inner
        + jnp.exp(cum)[:, :, :, None] * outer
        + skip_gain[:, None] * values.astype(jnp.float32)
    )
    ssm_out = ssm_out.reshape(slab_rows, columns)
    gated = ssm_out * jax.nn.silu(gate_in.astype(jnp.float32))
    span = INNER // GROUPS
    piece_len = min(columns, span)
    norm_here = columns // piece_len
    squares = jnp.sum((gated * gated).reshape(slab_rows, norm_here, piece_len), axis=2)
    norm_reach = span // piece_len
    for bit_index in range(norm_reach.bit_length() - 1):
        squares = squares + from_partner(squares, "tp", bit_index)
    scale = lax.rsqrt(squares / span + 1e-05)
    normed = (gated.reshape(slab_rows, norm_here, piece_len) * scale[:, :, None]).reshape(
        slab_rows, columns
    ) * norm_gain
    normed = normed.astype(jnp.bfloat16)
    return lax.psum_scatter(
        jnp.dot(normed, out_weight, preferred_element_type=jnp.float32).astype(jnp.bfloat16),
        "tp",
        scatter_dimension=0,
        tiled=True,
    )


def solution(mesh):
    return jax.shard_map(
        shards,
        mesh=mesh,
        in_specs=(
            P(("groups", "ctx", "tp"), None),
            P(None, "tp"),
            P(None, "tp"),
            P(None, "tp"),
            P(None, "tp"),
            P(None, "tp"),
            P(None, "tp"),
            P(None, "tp"),
            P(None, "tp"),
            P("tp"),
            P("tp"),
            P("tp"),
            P("tp"),
            P("tp", None),
        ),
        out_specs=P(("groups", "ctx", "tp"), None),
        check_vma=False,
    )
```

profile of v0, /device:TPU:19, one launch (start us, length us, event | category | flops | bytes accessed | tf_op | source)
XLA Modules:
  0.0 213.1 jit_solution(11843969532466054839)
XLA Ops:
  7.4 14.3 %constant_dynamic-update-slice_fusion.4 = bf16[4096,4640]{1,0:T(8,128)(2,1)} fusion(bf16[4096,2048]{1,0:T(8,128)(2,1)} %param.19), kind=kLoop, calls=%fused_computation.56 | loop fusion | bytes 33554432
  22.9 14.4 %constant_dynamic-update-slice_fusion.3 = bf16[4096,4640]{1,0:T(8,128)(2,1)} fusion(bf16[4096,4640]{1,0:T(8,128)(2,1)} %constant_dynamic-update-slice_fusion.4, bf16[4096,2048]{1,0:T(8,128)(2,1)} %param.20), kind=kLoop, calls=%fused_computation.55 | loop fusion | bytes 33554432
  37.3 1.6 constant_dynamic-update-slice_fusion.2
  39.7 1.6 constant_dynamic-update-slice_fusion.1
  42.4 12.2 %all-gather.2.cloned.1.call-done = bf16[256,4096]{1,0:T(8,128)(2,1)} async-done(((bf16[64,4096]{1,0:T(8,128)(2,1)}), bf16[256,4096]{1,0:T(8,128)(2,1)}) %all-gather.2.cloned.1.call-update) | async-done | bytes 2097168 | tf_op jit(solution)/shard_map/all_gather | solution.py:63
  54.6 20.0 %fusion.29 = (bf16[256,4640]{0,1:T(8,128)(2,1)}, f32[256,4640]{0,1:T(8,128)}) fusion(bf16[4096,4640]{1,0:T(8,128)(2,1)} %constant_dynamic-update-slice_fusion, bf16[256,4096]{1,0:T(8,128)(2,1)} %all-gather.2.cloned.1.call-done), kind=kOutput, calls=%fused_computation.73 | convolution fusion | flops 9731973120 | bytes 47235072 | tf_op jit(solution)/shard_map/dot_general | solution.py:62
  76.8 1.5 collective-permute-start
  80.9 1.4 slice.70
  82.8 1.6 copy.49
  84.4 1.9 copy.36
  86.3 1.9 maximum_convert_fusion
  88.3 4.0 %multiply_convert_fusion.1 = bf16[256,2560]{0,1:T(8,128)(2,1)S(1)} fusion(f32[259,2560]{0,1:T(8,128)S(1)} %maximum_convert_fusion, f32[2560]{0:T(1024)S(1)} %copy-done.10, f32[2560]{0:T(1024)S(1)} %copy-done.11, f32[2560]{0:T(1024)S(1)} %copy-done.12, f32[2560]{0:T(1024)S(1)} %get-tuple-element.89), kind=kLoop, calls=%fused_computation.21 | loop fusion | flops 7864320 | bytes 11837440 | tf_op jit(solution)/shard_map/convert_element_type | solution.py:71
  96.0 3.5 %fusion.19 = f32[2,32,128,64]{3,2,1,0:T(8,128)} fusion(bf16[2,128,32,128]{3,1,2,0:T(8,128)(2,1)S(1)} %bitcast.70, f32[2,128,32]{1,2,0:T(8,128)} %copy.49, bf16[2,128,32,64]{1,0,3,2:T(2,128)(2,1)S(1)} %reshape.64), kind=kOutput, calls=%fused_computation.41 | convolution fusion | flops 135790592 | bytes 5275648 | tf_op jit(solution)/shard_map/buhn,buhp->bhnp/dot_general | solution.py:113
  99.5 4.0 %while.24 = (s32[]{:T(128)}, f32[32,128,64]{2,1,0:T(8,128)S(1)}, f32[2,32]{1,0:T(2,128)S(1)}, f32[2,32,128,64]{3,2,1,0:T(8,128)}, s32[]{:T(128)}, /*index=5*/s32[]{:T(128)}) while((s32[]{:T(128)}, f32[32,128,64]{2,1,0:T(8,128)S(1)}, f32[2,32]{1,0:T(2,128)S(1)}, f32[2,32,128,64]{3,2,1,0:T(8,128)}, s32[]{:T(128)}, ...), condition=%wide.region_3.4_spmd.clone, body=%wide.region_2.3_spmd.clone.sunk | while | flops 786435 | bytes 3146199 | solution.py:121
  99.5 2.0 bitcast_add_fusion.5
  101.5 2.0 bitcast_add_fusion.5
  105.6 3.3 %collective-permute-done.1 = bf16[32,128,64]{1,2,0:T(8,128)(2,1)S(1)} collective-permute-done((bf16[32,128,64]{1,2,0:T(8,128)(2,1)S(1)}, bf16[32,128,64]{1,2,0:T(8,128)(2,1)S(1)}, u32[]{:S(2)}, u32[]{:S(2)}) %collective-permute-start.1) | collective-permute-done | bytes 524320 | tf_op jit(solution)/shard_map/ppermute | solution.py:14
  112.4 7.2 %collective-permute-done.2 = bf16[32,128,64]{1,2,0:T(8,128)(2,1)S(1)} collective-permute-done((bf16[32,128,64]{1,2,0:T(8,128)(2,1)S(1)}, bf16[32,128,64]{1,2,0:T(8,128)(2,1)S(1)}, u32[]{:S(2)}, u32[]{:S(2)}) %collective-permute-start.2) | collective-permute-done | bytes 524320 | tf_op jit(solution)/shard_map/ppermute | solution.py:14
  119.8 1.6 collective-permute-start.3
  122.2 3.3 %fusion.10 = f32[2,32,64,128]{3,2,1,0:T(8,128)} fusion(f32[32,2,128,128]{3,2,0,1:T(8,128)S(1)} %bitcast.72, f32[32,2,128]{2,0,1:T(8,128)S(1)} %copy.43, f32[32,2,128]{2,0,1:T(8,128)S(1)} %copy.41, pred[128,128]{1,0:T(8,128)(4,1)S(1)} %iota_compare_fusion, bf16[2,128,32,64]{1,0,3,2:T(2,128)(2,1)S(1)} %copy-done.3), kind=kOutput, calls=%fused_computation.28 | convolution fusion | flops 140509184 | bytes 7421952 | tf_op jit(solution)/shard_map/hbtu,buhp->bthp/dot_general | solution.py:108
  125.5 5.1 %collective-permute-done.3 = bf16[32,128,64]{1,2,0:T(8,128)(2,1)} collective-permute-done((bf16[32,128,64]{1,2,0:T(8,128)(2,1)S(1)}, bf16[32,128,64]{1,2,0:T(8,128)(2,1)}, u32[]{:S(2)}, u32[]{:S(2)}) %collective-permute-start.3) | collective-permute-done | bytes 524320 | tf_op jit(solution)/shard_map/ppermute | solution.py:14
  130.6 1.4 copy.54
  132.0 6.8 %while.23 = (s32[]{:T(128)}, f32[32,128,64]{2,1,0:T(8,128)S(1)}, f32[2,32,128,64]{3,2,1,0:T(8,128)}, f32[2,32]{1,0:T(2,128)S(1)}, f32[2,32,128,64]{3,2,1,0:T(8,128)}, /*index=5*/s32[]{:T(128)}) while((s32[]{:T(128)}, f32[32,128,64]{2,1,0:T(8,128)S(1)}, f32[2,32,128,64]{3,2,1,0:T(8,128)}, f32[2,32]{1,0:T(2,128)S(1)}, ...), condition=%wide.region_5.6_spmd, body=%wide.region_4.5_spmd.sunk | while | flops 524290 | bytes 14681065 | solution.py:128
  132.0 1.5 bitcast_dynamic-update-slice_fusion.2
  133.5 1.4 copy-done
  135.4 1.5 bitcast_dynamic-update-slice_fusion.2
  136.9 1.4 copy-done
  140.4 6.1 %fusion.5 = f32[2,128,32,64]{1,3,2,0:T(8,128)S(1)} fusion(f32[2,32,64,128]{3,2,1,0:T(8,128)S(1)} %copy-done.6, f32[2,32,128,64]{3,2,1,0:T(8,128)} %get-tuple-element.55, bf16[2,128,32,128]{3,1,2,0:T(8,128)(2,1)S(1)} %bitcast.71, f32[32]{0:T(128)S(1)} %copy-done.20, f32[2,128,32]{1,2,0:T(8,128)S(1)} %copy.45, bf16[2,128,32,64]{1,0,3,2:T(2,128)(2,1)S(1)} %copy-done.3), kind=kOutput, calls=%fused_computation.23 | convolution fusion | flops 807927808 | bytes 9470080 | tf_op jit(solution)/shard_map/bthn,bhnp->bthp/dot_general | solution.py:129
  146.5 1.7 copy.58
  148.2 1.9 bitcast_reduce_fusion
  150.5 5.7 %convolution_convert_fusion = bf16[256,4096]{1,0:T(8,128)(2,1)} fusion(bf16[256,2048]{0,1:T(8,128)(2,1)S(1)} %fusion.12, bf16[2048,4096]{1,0:T(8,128)(2,1)S(1)} %copy-done.1), kind=kOutput, calls=%fused_computation.8 | convolution fusion | flops 4296015872 | bytes 19922944 | tf_op jit(solution)/shard_map/dot_general | solution.py:152
  156.2 50.0 %reduce-scatter.2.cloned.1.call-done = bf16[64,4096]{1,0:T(8,128)(2,1)} async-done(((bf16[256,4096]{1,0:T(8,128)(2,1)}), bf16[64,4096]{1,0:T(8,128)(2,1)}) %reduce-scatter.2.cloned.1.call-update) | async-done | bytes 524304 | tf_op jit(solution)/shard_map/reduce_scatter | solution.py:151
  (100 shorter events, 22.2 us)
Async XLA Ops:
  6.5 48.0 %all-gather.2.cloned.1.call-start = ((), (), s32[]{:S(2)}) async-start(), calls=%async_computation.1 | async-start | bytes 2621440 | tf_op jit(solution)/shard_map/all_gather | solution.py:63
  7.3 14.4 %copy-start.13 = (f32[4,2048]{1,0:T(4,128)S(1)}, f32[4,2048]{1,0:T(4,128)}, u32[]{:S(2)}) copy-start(f32[4,2048]{1,0:T(4,128)} %param.24) | copy-start | bytes 98308
  7.3 14.4 %copy-start.15 = (f32[4,256]{1,0:T(4,128)S(1)}, f32[4,256]{1,0:T(4,128)}, u32[]{:S(2)}) copy-start(f32[4,256]{1,0:T(4,128)} %param.25) | copy-start | bytes 12292
  7.3 14.4 %copy-start.16 = (f32[4,256]{1,0:T(4,128)S(1)}, f32[4,256]{1,0:T(4,128)}, u32[]{:S(2)}) copy-start(f32[4,256]{1,0:T(4,128)} %param.26) | copy-start | bytes 12292
  7.3 14.4 %copy-start.9 = (bf16[4096,32]{0,1:T(8,128)(2,1)S(1)}, bf16[4096,32]{0,1:T(8,128)(2,1)}, u32[]{:S(2)}) copy-start(bf16[4096,32]{0,1:T(8,128)(2,1)} %param.23) | copy-start | bytes 786436
  7.3 15.6 %copy-start.22 = (f32[32]{0:T(128)S(1)}, f32[32]{0:T(128)}, u32[]{:S(2)}) copy-start(f32[32]{0:T(128)} %param.28) | copy-start | bytes 388
  7.3 199.0 %reduce-scatter.2.cloned.1.call-start = ((), (), s32[]{:S(2)}) async-start(), calls=%async_computation.2 | async-start | bytes 2621440 | tf_op jit(solution)/shard_map/reduce_scatter | solution.py:151
  22.9 14.4 %copy-start.4 = (bf16[4096,256]{1,0:T(8,128)(2,1)S(1)}, bf16[4096,256]{1,0:T(8,128)(2,1)}, u32[]{:S(2)}) copy-start(bf16[4096,256]{1,0:T(8,128)(2,1)} %param.21) | copy-start | bytes 6291460
  37.3 2.4 %copy-start.5 = (bf16[4096,256]{1,0:T(8,128)(2,1)S(1)}, bf16[4096,256]{1,0:T(8,128)(2,1)}, u32[]{:S(2)}) copy-start(bf16[4096,256]{1,0:T(8,128)(2,1)} %param.22) | copy-start | bytes 6291460
  42.4 35.9 %copy-start.19 = (f32[32]{0:T(128)S(1)}, f32[32]{0:T(128)}, u32[]{:S(2)}) copy-start(f32[32]{0:T(128)} %param.27) | copy-start | bytes 388
  76.8 7.6 %collective-permute-start = (bf16[3,2560]{1,0:T(4,128)(2,1)}, bf16[3,2560]{1,0:T(4,128)(2,1)}, u32[]{:S(2)}, u32[]{:S(2)}) collective-permute-start(bf16[3,2560]{1,0:T(4,128)(2,1)} %copy.35), channel_id=1, source_target_pairs={{0,4},{4,8},{8,12},{1,5},{5,9},{9,13},{2,6},{6,10},{10,14},{3,7},{... | collective-permute-start | bytes 46088 | tf_op jit(solution)/shard_map/ppermute | solution.py:14
  79.5 0.9 copy-start.8
  86.3 1.9 copy-start.10
  86.3 1.9 copy-start.11
  86.3 2.0 copy-start.12
  95.5 4.0 %copy-start.2 = (bf16[2,128,32,64]{1,0,3,2:T(2,128)(2,1)}, bf16[2,128,32,64]{1,0,3,2:T(2,128)(2,1)S(1)}, u32[]{:S(2)}) copy-start(bf16[2,128,32,64]{1,0,3,2:T(2,128)(2,1)S(1)} %reshape.64) | copy-start | bytes 3145732
  96.0 3.5 %copy-start.18 = (f32[2,32]{1,0:T(2,128)S(1)}, f32[2,32]{1,0:T(2,128)}, u32[]{:S(2)}) copy-start(f32[2,32]{1,0:T(2,128)} %exp.48) | copy-start | bytes 772
  103.5 0.6 copy-start.21
  103.5 5.4 %copy-start.17 = (f32[32]{0:T(128)S(1)}, f32[32]{0:T(128)}, u32[]{:S(2)}) copy-start(f32[32]{0:T(128)} %get-tuple-element.121) | copy-start | bytes 388
  104.1 7.2 %copy-start.7 = (f32[2,128,32]{2,1,0:T(8,128)S(1)}, f32[2,128,32]{2,1,0:T(8,128)}, u32[]{:S(2)}) copy-start(f32[2,128,32]{2,1,0:T(8,128)} %get-tuple-element.117) | copy-start | bytes 98308
  104.3 4.6 %collective-permute-start.1 = (bf16[32,128,64]{1,2,0:T(8,128)(2,1)S(1)}, bf16[32,128,64]{1,2,0:T(8,128)(2,1)S(1)}, u32[]{:S(2)}, u32[]{:S(2)}) collective-permute-start(bf16[32,128,64]{1,2,0:T(8,128)(2,1)S(1)} %add_convert_fusion.2), channel_id=1, source_target_pairs={{0,4},{4,8},{8,12},{1,5},{5,9},{9,13},{2,6},{6,10},{10,14},{3,7},{... | collective-permute-start | bytes 1572872 | tf_op jit(solution)/shard_map/ppermute | solution.py:14
  109.1 10.5 %collective-permute-start.2 = (bf16[32,128,64]{1,2,0:T(8,128)(2,1)S(1)}, bf16[32,128,64]{1,2,0:T(8,128)(2,1)S(1)}, u32[]{:S(2)}, u32[]{:S(2)}) collective-permute-start(bf16[32,128,64]{1,2,0:T(8,128)(2,1)S(1)} %add_convert_fusion.1), channel_id=1, source_target_pairs={{0,4},{4,8},{8,12},{1,5},{5,9},{9,13},{2,6},{6,10},{10,14},{3,7},{... | collective-permute-start | bytes 1572872 | tf_op jit(solution)/shard_map/ppermute | solution.py:14
  119.8 2.4 %copy-start.3 = (bf16[2,128,32,64]{1,0,3,2:T(2,128)(2,1)S(1)}, bf16[2,128,32,64]{1,0,3,2:T(2,128)(2,1)}, u32[]{:S(2)}) copy-start(bf16[2,128,32,64]{1,0,3,2:T(2,128)(2,1)} %copy-done.2) | copy-start | bytes 3145732
  119.8 10.8 %collective-permute-start.3 = (bf16[32,128,64]{1,2,0:T(8,128)(2,1)S(1)}, bf16[32,128,64]{1,2,0:T(8,128)(2,1)}, u32[]{:S(2)}, u32[]{:S(2)}) collective-permute-start(bf16[32,128,64]{1,2,0:T(8,128)(2,1)S(1)} %add_convert_fusion), channel_id=1, source_target_pairs={{0,4},{4,8},{8,12},{1,5},{5,9},{9,13},{2,6},{6,10},{10,14},{3,7},{... | collective-permute-start | bytes 1572872 | tf_op jit(solution)/shard_map/ppermute | solution.py:14
  132.0 7.3 %copy-start.20 = (f32[32]{0:T(128)S(1)}, f32[32]{0:T(128)}, u32[]{:S(2)}) copy-start(f32[32]{0:T(128)} %param.29) | copy-start | bytes 388
  132.0 2.9 %copy-start = (f32[2,32,128,64]{3,2,1,0:T(8,128)S(1)}, f32[2,32,128,64]{3,2,1,0:T(8,128)}, u32[]{:S(2)}) copy-start(f32[2,32,128,64]{3,2,1,0:T(8,128)} %get-tuple-element.215) | copy-start | bytes 6291460 | tf_op jit(solution)/shard_map/while
  135.4 2.9 %copy-start = (f32[2,32,128,64]{3,2,1,0:T(8,128)S(1)}, f32[2,32,128,64]{3,2,1,0:T(8,128)}, u32[]{:S(2)}) copy-start(f32[2,32,128,64]{3,2,1,0:T(8,128)} %get-tuple-element.215) | copy-start | bytes 6291460 | tf_op jit(solution)/shard_map/while
  138.8 1.6 copy-start.6
  140.4 10.1 %copy-start.1 = (bf16[2048,4096]{1,0:T(8,128)(2,1)S(1)}, bf16[2048,4096]{1,0:T(8,128)(2,1)}, u32[]{:S(2)}) copy-start(bf16[2048,4096]{1,0:T(8,128)(2,1)} %param.31) | copy-start | bytes 50331652
  148.2 2.0 copy-start.14
Sparse Core Ops, SparseCore 0:
  8.9 45.6 all-gather.1
  156.4 49.8 reduce-scatter.1
where the time goes:
time: 216 us; the launch traced here: 213 us
  waiting for transfers between devices  78.5 us (36%)
  local copies, waits for them, and re-layouts  60.2 us (28%)
  matrix products  38.8 us (18%)
  other arithmetic  15.9 us (7%)
  between operations  13.9 us (6%)
  starting transfers between devices  5.73 us (3%)
    reduce_scatter x1, waiting for transfers between devices, shards(): lax.psum_scatter(jnp.dot(normed, out_weight, preferred_element_type=jnp.f...  50 us
    unnamed x51, local copies, waits for them, and re-layouts  34.3 us
    dot_general x1, matrix products, shards(): jnp.dot(lax.all_gather(tokens, 'tp', axis=0, tiled=True), joined, preferr...  20 us
    ppermute x4, waiting for transfers between devices, passed_along(): return lax.ppermute(shard, axis, pairs)  15.6 us
    all_gather x1, waiting for transfers between devices, shards(): lax.all_gather(tokens, 'tp', axis=0, tiled=True)  12.2 us
    dot_general x1, matrix products, shards(): jnp.einsum('bthn,bhnp->bthp', query_heads.astype(jnp.float32), starts, pr...  6.11 us
    dot_general x1, matrix products, shards(): jnp.dot(normed, out_weight, preferred_element_type=jnp.float32)  5.71 us
    ppermute x4, starting transfers between devices, passed_along(): return lax.ppermute(shard, axis, pairs)  5.69 us
  transfers between devices with their start and end apart: 6, of which 5 were waited for; matrix products, arithmetic and copies ran while one was open for 22% of the time, Pallas kernels for 0%

commit v1 on v0

--- a/solution.py
+++ b/solution.py
@@ -1,6 +1,10 @@
+import functools
+
 import jax
 import jax.numpy as jnp
 from jax import lax
+from jax.experimental import pallas as pl
+from jax.experimental.pallas import tpu as pltpu
 from jax.sharding import PartitionSpec as P
 
 STATE = 128
@@ -156,9 +160,517 @@
     )
 
 
+TILE = 256
+BLOCK = 128
+MESH = pl.DeviceIdType.MESH
+EXACT = lax.Precision.HIGHEST
+
+
+def greet(neighbours):
+    barrier = pltpu.get_barrier_semaphore()
+    count = 0
+    for axis, index, exists in neighbours:
+
+        @pl.when(exists)
+        def _():
+            pl.semaphore_signal(barrier, inc=1, device_id={axis: index}, device_id_type=MESH)
+
+        count = count + exists.astype(jnp.int32)
+    pl.semaphore_wait(barrier, count)
+
+
+def project_kernel(
+    n, tiles, tokens, gate_w, value_w, key_w, query_w, step_w, pre, step_raw,
+    rows, weights, step_buf, weight_sem, step_sem, send_left, send_right, recv_sem,
+):
+    me = lax.axis_index("tp")
+    length = tokens.shape[0]
+    step_copy = pltpu.make_async_copy(step_w, step_buf, step_sem)
+    step_copy.start()
+    tile = 0
+    for source in (gate_w, value_w, key_w, query_w):
+        for part in range(source.shape[1] // TILE):
+            pltpu.make_async_copy(
+                source.at[:, pl.ds(part * TILE, TILE)], weights.at[tile], weight_sem.at[tile]
+            ).start()
+            tile += 1
+    rows[me] = tokens[...]
+    greet([("tp", me - 1, me > 0), ("tp", me + 1, me < n - 1)])
+
+    def rightward(chunk):
+        return pltpu.make_async_remote_copy(
+            src_ref=rows.at[chunk], dst_ref=rows.at[chunk],
+            send_sem=send_right.at[chunk], recv_sem=recv_sem.at[chunk],
+            device_id={"tp": me + 1}, device_id_type=MESH,
+        )
+
+    def leftward(chunk):
+        return pltpu.make_async_remote_copy(
+            src_ref=rows.at[chunk], dst_ref=rows.at[chunk],
+            send_sem=send_left.at[chunk], recv_sem=recv_sem.at[chunk],
+            device_id={"tp": me - 1}, device_id_type=MESH,
+        )
+
+    @pl.when(me < n - 1)
+    def _():
+        rightward(me).start()
+
+    @pl.when(me > 0)
+    def _():
+        leftward(me).start()
+
+    def multiply(chunk, first):
+        place = pl.ds(pl.multiple_of(chunk * length, length), length)
+
+        def one(t, _):
+            if first:
+                pltpu.make_async_copy(
+                    gate_w.at[:, pl.ds(0, TILE)], weights.at[t], weight_sem.at[t]
+                ).wait()
+            pre[t, place, :] = jnp.dot(
+                rows[chunk], weights[t], preferred_element_type=jnp.float32
+            ).astype(jnp.bfloat16)
+            return 0
+
+        lax.fori_loop(0, tiles, one, 0)
+        step_raw[place, :] = jnp.dot(
+            rows[chunk], step_buf[...], preferred_element_type=jnp.float32
+        )
+
+    step_copy.wait()
+    multiply(me, True)
+    for far in range(1, n):
+        below, above = me - far, me + far
+
+        @pl.when(below >= 0)
+        def _():
+            rightward(below).wait_recv()
+
+            @pl.when(me < n - 1)
+            def _():
+                rightward(below).start()
+
+        @pl.when(above < n)
+        def _():
+            leftward(above).wait_recv()
+
+            @pl.when(me > 0)
+            def _():
+                leftward(above).start()
+
+        @pl.when(below >= 0)
+        def _():
+            multiply(below, False)
+
+        @pl.when(above < n)
+        def _():
+            multiply(above, False)
+
+    for chunk in range(n):
+
+        @pl.when(jnp.logical_and(chunk <= me, me < n - 1))
+        def _():
+            rightward(chunk).wait_send()
+
+        @pl.when(jnp.logical_and(chunk >= me, me > 0))
+        def _():
+            leftward(chunk).wait_send()
+
+
+def silu(v):
+    return v / (1.0 + jnp.exp(-v))
+
+
+def layer_kernel(
+    n, slabs, value_tiles, key_tiles,
+    pre, step_raw, value_conv, key_conv, query_conv, step_bias, decay_log, skip_gain, norm_gain, out_w,
+    out,
+    border, edge_buf, padded, keys, queries, scores, acts, cum_s, cum_t, step_t, tail_s, grow_s,
+    grow_x, local0, slab, leaving, inflow, gated, squares, normed, weight, partial, from_left, from_right,
+    edge_send, edge_recv, state_send, state_recv, weight_sem, part_send, left_recv, right_recv,
+):
+    me = lax.axis_index("tp")
+    ctx = lax.axis_index("ctx")
+    slab_rows, heads = step_raw.shape
+    blocks = slab_rows // BLOCK
+    length = slab_rows // n
+    kernel_len = value_conv.shape[0]
+    conv_tiles = value_tiles + 2 * key_tiles
+    group_tiles = INNER // GROUPS // TILE
+    width = TILE // (value_tiles * TILE // heads)
+    last = slab_rows - 16
+    pieces = partial.shape[1]
+    piece = partial.shape[3]
+    weight_copy = pltpu.make_async_copy(out_w, weight, weight_sem)
+    weight_copy.start()
+    for t in range(conv_tiles):
+        edge_buf[t] = pre[value_tiles + t, pl.ds(last, 16), :]
+    greet([
+        ("tp", me - 1, me > 0), ("tp", me + 1, me < n - 1),
+        ("ctx", ctx - 1, ctx > 0), ("ctx", ctx + 1, ctx < slabs - 1),
+    ])
+    edge = pltpu.make_async_remote_copy(
+        src_ref=edge_buf, dst_ref=border, send_sem=edge_send, recv_sem=edge_recv,
+        device_id={"ctx": ctx + 1}, device_id_type=MESH,
+    )
+
+    @pl.when(ctx < slabs - 1)
+    def _():
+        edge.start()
+
+    @pl.when(ctx == 0)
+    def _():
+        border[...] = jnp.zeros_like(border)
+        inflow[...] = jnp.zeros_like(inflow)
+
+    row = lax.broadcasted_iota(jnp.int32, (BLOCK, BLOCK), 0)
+    col = lax.broadcasted_iota(jnp.int32, (BLOCK, BLOCK), 1)
+    causal = row >= col
+    lower = jnp.where(causal, 1.0, 0.0)
+    upper = jnp.where(row <= col, 1.0, 0.0)
+    same = jnp.where(row == col, 1.0, 0.0)
+    turned = (((0,), (0,)), ((), ()))
+    raw = step_raw[...] + step_bias[...]
+    step = jnp.maximum(raw, 0.0) + jnp.log1p(jnp.exp(-jnp.abs(raw)))
+    rate = -jnp.exp(decay_log[...]) * step
+    for b in range(blocks):
+        lo = b * BLOCK
+        rate_b, step_b = rate[lo:lo + BLOCK], step[lo:lo + BLOCK]
+        cum = jnp.dot(lower, rate_b, precision=EXACT, preferred_element_type=jnp.float32)
+        cum_s[pl.ds(lo, BLOCK), :] = cum
+        cum_t[b] = lax.dot_general(rate_b, upper, turned, precision=EXACT, preferred_element_type=jnp.float32)
+        step_t[b] = lax.dot_general(step_b, same, turned, precision=EXACT, preferred_element_type=jnp.float32)
+        tail_s[pl.ds(lo, BLOCK), :] = jnp.exp(cum[BLOCK - 1:BLOCK] - cum) * step_b
+        grow_s[pl.ds(lo, BLOCK), :] = jnp.exp(cum)
+
+    def convolve(t, taps):
+        padded[pl.ds(0, 16), :] = border[t].astype(jnp.float32)
+        padded[pl.ds(16, slab_rows), :] = pre[value_tiles + t].astype(jnp.float32)
+        total = padded[pl.ds(17 - kernel_len, slab_rows), :] * taps[0:1]
+        for k in range(1, kernel_len):
+            total = total + padded[pl.ds(17 - kernel_len + k, slab_rows), :] * taps[k:k + 1]
+        return silu(total).astype(jnp.bfloat16)
+
+    @pl.when(ctx > 0)
+    def _():
+        edge.wait_recv()
+
+    per_tile = TILE // STATE
+    for t in range(key_tiles):
+        cols = slice(t * TILE, (t + 1) * TILE)
+        key = convolve(value_tiles + t, key_conv[:, cols])
+        query = convolve(value_tiles + key_tiles + t, query_conv[:, cols])
+        for g in range(per_tile):
+            keys[t * per_tile + g] = key[:, g * STATE:(g + 1) * STATE]
+            queries[t * per_tile + g] = query[:, g * STATE:(g + 1) * STATE]
+    for g in range(key_tiles * per_tile):
+        for b in range(blocks):
+            lo = b * BLOCK
+            scores[g, b] = lax.dot_general(
+                queries[g, pl.ds(lo, BLOCK), :], keys[g, pl.ds(lo, BLOCK), :],
+                (((1,), (1,)), ((), ())), preferred_element_type=jnp.float32,
+            )
+
+    def spread(t, each, count):
+        head = lax.broadcasted_iota(jnp.int32, (heads, each * count), 0)
+        lane = lax.broadcasted_iota(jnp.int32, (heads, each * count), 1)
+        return jnp.where(head == t * count + lane // each, 1.0, 0.0)
+
+    def widen(array, matrix):
+        return jnp.dot(array, matrix, precision=EXACT, preferred_element_type=jnp.float32)
+
+    def state_copy(t):
+        return pltpu.make_async_remote_copy(
+            src_ref=leaving.at[t], dst_ref=inflow.at[t],
+            send_sem=state_send.at[t], recv_sem=state_recv.at[t],
+            device_id={"ctx": ctx + 1}, device_id_type=MESH,
+        )
+
+    def first_pass(t, _):
+        place = pl.ds(pl.multiple_of(t * TILE, TILE), TILE)
+        value = convolve(t, value_conv[:, place])
+        acts[t] = value
+        chooser = spread(t, TILE // width, width)
+        tail = widen(tail_s[...], chooser)
+        grow = widen(grow_s[...], chooser)
+        grow_x[t] = grow
+        weighted = (value.astype(jnp.float32) * tail).astype(jnp.bfloat16)
+        g = t // group_tiles
+        state = jnp.zeros((STATE, TILE), jnp.float32)
+        for b in range(blocks):
+            lo = b * BLOCK
+            added = lax.dot_general(
+                keys[g, pl.ds(lo, BLOCK), :], weighted[lo:lo + BLOCK], turned,
+                preferred_element_type=jnp.float32,
+            )
+            state = grow[lo + BLOCK - 1:lo + BLOCK] * state + added
+            if b < blocks - 1:
+                local0[b, t] = state
+        slab[t] = state
+
+        @pl.when(ctx == 0)
+        def _():
+            leaving[t] = state.astype(jnp.bfloat16)
+            if slabs > 1:
+                state_copy(t).start()
+
+        return 0
+
+    lax.fori_loop(0, value_tiles, first_pass, 0)
+    squares[...] = jnp.zeros_like(squares)
+    left_half = lax.broadcasted_iota(jnp.int32, (BLOCK, BLOCK), 1) < TILE // width
+
+    def second_pass(t, _):
+        grow = grow_x[t]
+
+        @pl.when(ctx > 0)
+        def _():
+            state_copy(t).wait_recv()
+
+        start = inflow[t].astype(jnp.float32)
+        fall = jnp.ones((1, TILE), jnp.float32)
+        falls = []
+        for b in range(blocks):
+            falls.append(fall)
+            fall = fall * grow[(b + 1) * BLOCK - 1:(b + 1) * BLOCK]
+
+        @pl.when(jnp.logical_and(ctx > 0, ctx < slabs - 1))
+        def _():
+            leaving[t] = (fall * start + slab[t]).astype(jnp.bfloat16)
+            state_copy(t).start()
+
+        g = t // group_tiles
+        columns = widen(cum_s[...], spread(t, BLOCK, width))
+        place = pl.ds(pl.multiple_of(t * TILE, TILE), TILE)
+        skip = widen(jnp.broadcast_to(skip_gain[...], (8, heads)), spread(t, TILE // width, width))[0:1]
+        for b in range(blocks):
+            lo = b * BLOCK
+            value = acts[t, pl.ds(lo, BLOCK), :]
+            parts = []
+            for pair in range(width // 2):
+                both = []
+                for k in (2 * pair, 2 * pair + 1):
+                    h = t * width + k
+                    diff = columns[lo:lo + BLOCK, k * BLOCK:(k + 1) * BLOCK] - cum_t[b, pl.ds(h, 1), :]
+                    factor = jnp.exp(jnp.where(causal, diff, -1e30))
+                    mix = (scores[g, b] * factor * step_t[b, pl.ds(h, 1), :]).astype(jnp.bfloat16)
+                    both.append(jnp.dot(
+                        mix, value[:, pair * BLOCK:(pair + 1) * BLOCK], preferred_element_type=jnp.float32
+                    ))
+                parts.append(jnp.where(left_half, both[0], both[1]))
+            inner = jnp.concatenate(parts, axis=1)
+            enter = start if b == 0 else falls[b] * start + local0[b - 1, t]
+            outer = jnp.dot(
+                queries[g, pl.ds(lo, BLOCK), :], enter.astype(jnp.bfloat16), preferred_element_type=jnp.float32
+            )
+            ssm = inner + grow[lo:lo + BLOCK] * outer + skip * value.astype(jnp.float32)
+            gate = pre[t, pl.ds(lo, BLOCK), :].astype(jnp.float32)
+            result = ssm * silu(gate)
+            gated[t, pl.ds(lo, BLOCK), :] = result
+            squares[g, pl.ds(lo, BLOCK), :] += result * result
+        return 0
+
+    lax.fori_loop(0, value_tiles, second_pass, 0)
+    groups_here = value_tiles // group_tiles
+    for g in range(groups_here):
+        scale = lax.rsqrt(jnp.sum(squares[g], axis=1, keepdims=True) / (INNER // GROUPS) + 1e-05)
+        for t in range(g * group_tiles, (g + 1) * group_tiles):
+            cols = slice(t * TILE, (t + 1) * TILE)
+            normed[:, cols] = (gated[t] * scale * norm_gain[:, cols]).astype(jnp.bfloat16)
+
+    weight_copy.wait()
+
+    def product(b, p):
+        rows = normed[pl.ds(pl.multiple_of(b * length, length), length), :]
+        return jnp.dot(
+            rows, weight[:, pl.ds(pl.multiple_of(p * piece, piece), piece)],
+            preferred_element_type=jnp.float32,
+        )
+
+    def rightward(b, p):
+        return pltpu.make_async_remote_copy(
+            src_ref=partial.at[b, p], dst_ref=from_left.at[b, p],
+            send_sem=part_send.at[b, p], recv_sem=left_recv.at[b, p],
+            device_id={"tp": me + 1}, device_id_type=MESH,
+        )
+
+    def leftward(b, p):
+        return pltpu.make_async_remote_copy(
+            src_ref=partial.at[b, p], dst_ref=from_right.at[b, p],
+            send_sem=part_send.at[b, p], recv_sem=right_recv.at[b, p],
+            device_id={"tp": me - 1}, device_id_type=MESH,
+        )
+
+    for far in range(n - 1, 0, -1):
+        above, below = me + far, me - far
+
+        def forward(p, _):
+            @pl.when(above < n)
+            def _():
+                mine = product(above, p)
+
+                @pl.when(me == 0)
+                def _():
+                    partial[above, p] = mine.astype(jnp.bfloat16)
+
+                @pl.when(me > 0)
+                def _():
+                    rightward(above, p).wait_recv()
+                    partial[above, p] = (
+                        mine + from_left[above, p].astype(jnp.float32)
+                    ).astype(jnp.bfloat16)
+
+                rightward(above, p).start()
+
+            @pl.when(below >= 0)
+            def _():
+                mine = product(below, p)
+
+                @pl.when(me == n - 1)
+                def _():
+                    partial[below, p] = mine.astype(jnp.bfloat16)
+
+                @pl.when(me < n - 1)
+                def _():
+                    leftward(below, p).wait_recv()
+                    partial[below, p] = (
+                        mine + from_right[below, p].astype(jnp.float32)
+                    ).astype(jnp.bfloat16)
+
+                leftward(below, p).start()
+
+            return 0
+
+        lax.fori_loop(0, pieces, forward, 0)
+
+    for p in range(pieces):
+        cols = pl.ds(p * piece, piece)
+        partial[me, p] = product(me, p).astype(jnp.bfloat16)
+
+    @pl.when(me == 0)
+    def _():
+        from_left[me] = jnp.zeros(from_left.shape[1:], from_left.dtype)
+
+    @pl.when(me == n - 1)
+    def _():
+        from_right[me] = jnp.zeros(from_right.shape[1:], from_right.dtype)
+
+    for p in range(pieces):
+        cols = pl.ds(p * piece, piece)
+
+        @pl.when(me > 0)
+        def _():
+            rightward(me, p).wait_recv()
+
+        @pl.when(me < n - 1)
+        def _():
+            leftward(me, p).wait_recv()
+
+        out[:, cols] = (
+            partial[me, p].astype(jnp.float32)
+            + from_left[me, p].astype(jnp.float32)
+            + from_right[me, p].astype(jnp.float32)
+        ).astype(out.dtype)
+
+    for b in range(n):
+
+        @pl.when(b != me)
+        def _():
+            for p in range(pieces):
+                rightward(b, p).wait_send()
+
+    @pl.when(ctx < slabs - 1)
+    def _():
+        edge.wait_send()
+        for t in range(value_tiles):
+            state_copy(t).wait_send()
+
+
+def fused(n, slabs, tokens, gate_weight, value_weight, key_weight, query_weight, step_weight,
+          value_conv, key_conv, query_conv, step_bias, decay_log, skip_gain, norm_gain, out_weight):
+    length, depth = tokens.shape
+    columns = gate_weight.shape[1]
+    key_cols = key_weight.shape[1]
+    heads = step_weight.shape[1]
+    slab_rows = length * n
+    value_tiles, key_tiles = columns // TILE, key_cols // TILE
+    tiles = 2 * value_tiles + 2 * key_tiles
+    bf16, f32 = jnp.bfloat16, jnp.float32
+    vmem, anywhere = pl.BlockSpec(memory_space=pltpu.VMEM), pl.BlockSpec(memory_space=pl.ANY)
+    dma = pltpu.SemaphoreType.DMA
+    pre, step_raw = pl.pallas_call(
+        functools.partial(project_kernel, n, tiles),
+        out_shape=(
+            jax.ShapeDtypeStruct((tiles, slab_rows, TILE), bf16),
+            jax.ShapeDtypeStruct((slab_rows, heads), f32),
+        ),
+        in_specs=[vmem] + [anywhere] * 5,
+        out_specs=(vmem, vmem),
+        scratch_shapes=[
+            pltpu.VMEM((n, length, depth), bf16),
+            pltpu.VMEM((tiles, depth, TILE), bf16),
+            pltpu.VMEM((depth, heads), bf16),
+            dma((tiles,)), dma, dma((n,)), dma((n,)), dma((n,)),
+        ],
+        compiler_params=pltpu.CompilerParams(
+            collective_id=0, has_side_effects=True, vmem_limit_bytes=56 * 2**20
+        ),
+    )(tokens, gate_weight, value_weight, key_weight, query_weight, step_weight)
+    blocks = slab_rows // BLOCK
+    groups_here = key_cols // STATE
+    out_cols = out_weight.shape[1]
+    piece = 1024
+    pieces = out_cols // piece
+    wide = (value_tiles, slab_rows, TILE)
+    conv_tiles = value_tiles + 2 * key_tiles
+    return pl.pallas_call(
+        functools.partial(layer_kernel, n, slabs, value_tiles, key_tiles),
+        out_shape=jax.ShapeDtypeStruct((length, out_cols), bf16),
+        in_specs=[vmem] * 9 + [anywhere],
+        out_specs=vmem,
+        scratch_shapes=[
+            pltpu.VMEM((conv_tiles, 16, TILE), bf16),
+            pltpu.VMEM((conv_tiles, 16, TILE), bf16),
+            pltpu.VMEM((slab_rows + 16, TILE), f32),
+            pltpu.VMEM((groups_here, slab_rows, STATE), bf16),
+            pltpu.VMEM((groups_here, slab_rows, STATE), bf16),
+            pltpu.VMEM((groups_here, blocks, BLOCK, BLOCK), f32),
+            pltpu.VMEM(wide, bf16),
+            pltpu.VMEM((slab_rows, heads), f32),
+            pltpu.VMEM((blocks, heads, BLOCK), f32),
+            pltpu.VMEM((blocks, heads, BLOCK), f32),
+            pltpu.VMEM((slab_rows, heads), f32),
+            pltpu.VMEM((slab_rows, heads), f32),
+            pltpu.VMEM(wide, f32),
+            pltpu.VMEM((max(blocks - 1, 1), value_tiles, STATE, TILE), f32),
+            pltpu.VMEM((value_tiles, STATE, TILE), f32),
+            pltpu.VMEM((value_tiles, STATE, TILE), bf16),
+            pltpu.VMEM((value_tiles, STATE, TILE), bf16),
+            pltpu.VMEM(wide, f32),
+            pltpu.VMEM((groups_here, slab_rows, TILE), f32),
+            pltpu.VMEM((slab_rows, columns), bf16),
+            pltpu.VMEM(out_weight.shape, bf16),
+            pltpu.VMEM((n, pieces, length, piece), bf16),
+            pltpu.VMEM((n, pieces, length, piece), bf16),
+            pltpu.VMEM((n, pieces, length, piece), bf16),
+            dma, dma, dma((value_tiles,)), dma((value_tiles,)), dma,
+            dma((n, pieces)), dma((n, pieces)), dma((n, pieces)),
+        ],
+        compiler_params=pltpu.CompilerParams(
+            collective_id=1, has_side_effects=True, vmem_limit_bytes=56 * 2**20
+        ),
+    )(
+        pre, step_raw, value_conv, key_conv, query_conv, step_bias[None], decay_log[None],
+        skip_gain[None], norm_gain[None], out_weight,
+    )
+
+
 def solution(mesh):
+    n, slabs = mesh.shape["tp"], mesh.shape["ctx"]
+    whole_groups = INNER // n % (INNER // GROUPS) == 0 and GROUPS * STATE // n % TILE == 0
+    body = functools.partial(fused, n, slabs) if whole_groups and n >= 4 else shards
     return jax.shard_map(
-        shards,
+        body,
         mesh=mesh,
         in_specs=(
             P(("groups", "ctx", "tp"), None),

time: 216 us -> 127 us (0.59); the launches traced: 213 us -> 127 us
  Pallas kernels: 0 us -> 123 us
  waiting for transfers between devices: 78.5 us -> 0 us
  local copies, waits for them, and re-layouts: 60.2 us -> 4.13 us
  matrix products: 38.8 us -> 0 us
  other arithmetic: 15.9 us -> 0 us
  between operations: 13.9 us -> 0.02 us
  starting transfers between devices: 5.73 us -> 0 us
    pallas_call x0 -> x2, Pallas kernels: none -> 123 us  [the longest x1 70.7 us: fused(): pl.pallas_call(functools.partial(layer_kernel, n, slabs, value_tiles, key...]
    reduce_scatter x1 -> x0, waiting for transfers between devices: 50 us -> none  [shards(): lax.psum_scatter(jnp.dot(normed, out_weight, preferred_element_type=jnp.f...]
    dot_general x6 -> x0, matrix products: 38.8 us -> none  [the longest x1 20 us: shards(): jnp.dot(lax.all_gather(tokens, 'tp', axis=0, tiled=True), joined, preferr...]
    unnamed x51 -> x2, local copies, waits for them, and re-layouts: 34.3 us -> 4.13 us
    ppermute x4 -> x0, waiting for transfers between devices: 15.6 us -> none  [passed_along(): return lax.ppermute(shard, axis, pairs)]
    all_gather x1 -> x0, waiting for transfers between devices: 12.2 us -> none  [shards(): lax.all_gather(tokens, 'tp', axis=0, tiled=True)]
    convert_element_type x6 -> x0, other arithmetic: 6.78 us -> none  [the longest x1 3.96 us: shards(): jax.nn.silu(causal_mix(padded, kernel, slab_rows)).astype(jnp.bfloat16)]
    slice x6 -> x0, local copies, waits for them, and re-layouts: 6.03 us -> none  [the longest x2 2.21 us: shards(): border = passed_along(mixed_pre[slab_rows - (kernel_len - 1):], 'ctx', 1)]
  transfers between devices with their start and end apart: 6 -> 0, of which waited for: 5 -> 0; matrix products, arithmetic and copies ran while one was open for 22% -> 0% of each run, Pallas kernels for 0% -> 0%
where the time goes in v1:
time: 127 us
  Pallas kernels  123 us (97%)
  local copies, waits for them, and re-layouts  4.13 us (3%)
    pallas_call x1, Pallas kernels, fused(): pl.pallas_call(functools.partial(layer_kernel, n, slabs, value_tiles, key...  70.7 us
    pallas_call x1, Pallas kernels, fused(): pl.pallas_call(functools.partial(project_kernel, n, tiles), out_shape=(ja...  52.3 us
    unnamed x2, local copies, waits for them, and re-layouts  4.13 us

profile of v1, /device:TPU:19, one launch (start us, length us, event | category | flops | bytes accessed | tf_op | source)
XLA Modules:
  0.0 127.1 jit_solution(12898385257516392803)
XLA Ops:
  0.0 2.3 %copy.15.step_w = bf16[4096,32]{1,0:T(8,128)(2,1)} copy(bf16[4096,32]{0,1:T(8,128)(2,1)} %param.19) | data formatting | bytes 524288 | tf_op args[5]
  2.3 52.3 %shard_map.136 = (bf16[18,256,256]{2,1,0:T(8,128)(2,1)}, f32[256,32]{1,0:T(8,128)}) custom-call(bf16[64,4096]{1,0:T(8,128)(2,1)} %tokens.1, bf16[4096,2048]{1,0:T(8,128)(2,1)} %gate_w.1, bf16[4096,2048]{1,0:T(8,128)(2,1)} %value_w.1, bf16[4096,256]{1,0:T(8,128)(2,1)} %key_w.1, bf16[4096,256]{1,0:T(8,128)(2,1)} %query_w.1, bf16[4096,32]{1,0:T(8,128)(2,1)} %copy.15.step_w), custom_call_target="tpu_custom_call" | custom-call | tf_op jit(solution)/shard_map/pallas_call | solution.py:601
  54.6 70.7 %shard_map.137 = bf16[64,4096]{1,0:T(8,128)(2,1)} custom-call(bf16[18,256,256]{2,1,0:T(8,128)(2,1)} %get-tuple-element.7.pre, f32[256,32]{1,0:T(8,128)} %get-tuple-element.8.step_raw, f32[4,2048]{1,0:T(4,128)} %value_conv.1, f32[4,256]{1,0:T(4,128)} %key_conv.1, f32[4,256]{1,0:T(4,128)} %query_conv.1, f32[1,32]{1,0:T(1,128)} %bitcast.5, f32[1,32]{1,0:T(1,128)} %bitcast.6, ...), custom_call_target="tpu_custom_call" | custom-call | tf_op jit(solution)/shard_map/pallas_call | solution.py:626
  125.3 1.9 %copy.17 = bf16[64,4096]{1,0:T(8,128)(2,1)} copy(bf16[64,4096]{1,0:T(8,128)(2,1)} %shard_map.137) | data formatting | bytes 1048576

commit v2 on v1

--- a/solution.py
+++ b/solution.py
@@ -180,105 +180,131 @@
 
 
 def project_kernel(
-    n, tiles, tokens, gate_w, value_w, key_w, query_w, step_w, pre, step_raw,
-    rows, weights, step_buf, weight_sem, step_sem, send_left, send_right, recv_sem,
+    n, tiles, quarters, tokens, gate_w, value_w, key_w, query_w, step_w, pre, step_raw,
+    rows, weights, step_buf, total, step_total,
+    weight_sem, step_sem, send_left, send_right, recv_sem,
 ):
     me = lax.axis_index("tp")
-    length = tokens.shape[0]
+    length, depth = tokens.shape
+    deep = depth // quarters
     step_copy = pltpu.make_async_copy(step_w, step_buf, step_sem)
     step_copy.start()
-    tile = 0
-    for source in (gate_w, value_w, key_w, query_w):
-        for part in range(source.shape[1] // TILE):
-            pltpu.make_async_copy(
-                source.at[:, pl.ds(part * TILE, TILE)], weights.at[tile], weight_sem.at[tile]
-            ).start()
-            tile += 1
-    rows[me] = tokens[...]
+    for q in range(quarters):
+        tile = 0
+        for source in (gate_w, value_w, key_w, query_w):
+            for part in range(source.shape[1] // TILE):
+                pltpu.make_async_copy(
+                    source.at[pl.ds(q * deep, deep), pl.ds(part * TILE, TILE)],
+                    weights.at[q, tile], weight_sem.at[q, tile],
+                ).start()
+                tile += 1
+
+    def place(chunk):
+        return pl.ds(pl.multiple_of(chunk * length, length), length)
+
+    for q in range(quarters):
+        rows[q, place(me), :] = tokens[:, q * deep:(q + 1) * deep]
     greet([("tp", me - 1, me > 0), ("tp", me + 1, me < n - 1)])
 
-    def rightward(chunk):
+    def rightward(q, chunk):
+        spot = rows.at[q, place(chunk)]
         return pltpu.make_async_remote_copy(
-            src_ref=rows.at[chunk], dst_ref=rows.at[chunk],
-            send_sem=send_right.at[chunk], recv_sem=recv_sem.at[chunk],
+            src_ref=spot, dst_ref=spot,
+            send_sem=send_right.at[q, chunk], recv_sem=recv_sem.at[q, chunk],
             device_id={"tp": me + 1}, device_id_type=MESH,
         )
 
-    def leftward(chunk):
+    def leftward(q, chunk):
+        spot = rows.at[q, place(chunk)]
         return pltpu.make_async_remote_copy(
-            src_ref=rows.at[chunk], dst_ref=rows.at[chunk],
-            send_sem=send_left.at[chunk], recv_sem=recv_sem.at[chunk],
+            src_ref=spot, dst_ref=spot,
+            send_sem=send_left.at[q, chunk], recv_sem=recv_sem.at[q, chunk],
             device_id={"tp": me - 1}, device_id_type=MESH,
         )
 
-    @pl.when(me < n - 1)
-    def _():
-        rightward(me).start()
-
-    @pl.when(me > 0)
-    def _():
-        leftward(me).start()
-
-    def multiply(chunk, first):
-        place = pl.ds(pl.multiple_of(chunk * length, length), length)
-
-        def one(t, _):
-            if first:
-                pltpu.make_async_copy(
-                    gate_w.at[:, pl.ds(0, TILE)], weights.at[t], weight_sem.at[t]
-                ).wait()
-            pre[t, place, :] = jnp.dot(
-                rows[chunk], weights[t], preferred_element_type=jnp.float32
-            ).astype(jnp.bfloat16)
-            return 0
-
-        lax.fori_loop(0, tiles, one, 0)
-        step_raw[place, :] = jnp.dot(
-            rows[chunk], step_buf[...], preferred_element_type=jnp.float32
-        )
-
-    step_copy.wait()
-    multiply(me, True)
-    for far in range(1, n):
+    for q in range(quarters):
+
+        @pl.when(me < n - 1)
+        def _():
+            rightward(q, me).start()
+
+        @pl.when(me > 0)
+        def _():
+            leftward(q, me).start()
+
+    def receive(q, far):
         below, above = me - far, me + far
 
         @pl.when(below >= 0)
         def _():
-            rightward(below).wait_recv()
+            rightward(q, below).wait_recv()
 
             @pl.when(me < n - 1)
             def _():
-                rightward(below).start()
+                rightward(q, below).start()
 
         @pl.when(above < n)
         def _():
-            leftward(above).wait_recv()
+            leftward(q, above).wait_recv()
 
             @pl.when(me > 0)
             def _():
-                leftward(above).start()
-
-        @pl.when(below >= 0)
-        def _():
-            multiply(below, False)
-
-        @pl.when(above < n)
-        def _():
-            multiply(above, False)
-
-    for chunk in range(n):
-
-        @pl.when(jnp.logical_and(chunk <= me, me < n - 1))
-        def _():
-            rightward(chunk).wait_send()
-
-        @pl.when(jnp.logical_and(chunk >= me, me > 0))
-        def _():
-            leftward(chunk).wait_send()
+                leftward(q, above).start()
+
+    for far in range(1, n - 1):
+        for q in range(quarters):
+            receive(q, far)
+    step_copy.wait()
+    for q in range(quarters):
+        receive(q, n - 1)
+
+        def one(t, _):
+            pltpu.make_async_copy(
+                gate_w.at[pl.ds(0, deep), pl.ds(0, TILE)], weights.at[q, t], weight_sem.at[q, t]
+            ).wait()
+            added = jnp.dot(rows[q], weights[q, t], preferred_element_type=jnp.float32)
+            if q > 0:
+                added = total[t] + added
+            if q < quarters - 1:
+                total[t] = added
+            else:
+                pre[t] = added.astype(jnp.bfloat16)
+            return 0
+
+        lax.fori_loop(0, tiles, one, 0)
+        added = lax.dot_general(
+            rows[q], step_buf[:, q * deep:(q + 1) * deep], (((1,), (1,)), ((), ())),
+            preferred_element_type=jnp.float32,
+        )
+        if q > 0:
+            added = step_total[...] + added
+        if q < quarters - 1:
+            step_total[...] = added
+        else:
+            step_raw[...] = added
+
+    for q in range(quarters):
+        for chunk in range(n):
+
+            @pl.when(jnp.logical_and(chunk <= me, me < n - 1))
+            def _():
+                rightward(q, chunk).wait_send()
+
+            @pl.when(jnp.logical_and(chunk >= me, me > 0))
+            def _():
+                leftward(q, chunk).wait_send()
 
 
 def silu(v):
     return v / (1.0 + jnp.exp(-v))
+
+
+def three_parts(array):
+    high = array.astype(jnp.bfloat16)
+    rest = array - high.astype(jnp.float32)
+    middle = rest.astype(jnp.bfloat16)
+    low = (rest - middle.astype(jnp.float32)).astype(jnp.bfloat16)
+    return jnp.concatenate([high, middle, low], axis=1)
 
 
 def layer_kernel(
@@ -337,11 +363,11 @@
         lo = b * BLOCK
         rate_b, step_b = rate[lo:lo + BLOCK], step[lo:lo + BLOCK]
         cum = jnp.dot(lower, rate_b, precision=EXACT, preferred_element_type=jnp.float32)
-        cum_s[pl.ds(lo, BLOCK), :] = cum
+        cum_s[pl.ds(lo, BLOCK), :] = three_parts(cum)
         cum_t[b] = lax.dot_general(rate_b, upper, turned, precision=EXACT, preferred_element_type=jnp.float32)
         step_t[b] = lax.dot_general(step_b, same, turned, precision=EXACT, preferred_element_type=jnp.float32)
-        tail_s[pl.ds(lo, BLOCK), :] = jnp.exp(cum[BLOCK - 1:BLOCK] - cum) * step_b
-        grow_s[pl.ds(lo, BLOCK), :] = jnp.exp(cum)
+        tail_s[pl.ds(lo, BLOCK), :] = three_parts(jnp.exp(cum[BLOCK - 1:BLOCK] - cum) * step_b)
+        grow_s[pl.ds(lo, BLOCK), :] = three_parts(jnp.exp(cum))
 
     def convolve(t, taps):
         padded[pl.ds(0, 16), :] = border[t].astype(jnp.float32)
@@ -372,12 +398,12 @@
             )
 
     def spread(t, each, count):
-        head = lax.broadcasted_iota(jnp.int32, (heads, each * count), 0)
-        lane = lax.broadcasted_iota(jnp.int32, (heads, each * count), 1)
-        return jnp.where(head == t * count + lane // each, 1.0, 0.0)
+        head = lax.broadcasted_iota(jnp.int32, (3 * heads, each * count), 0) % heads
+        lane = lax.broadcasted_iota(jnp.int32, (3 * heads, each * count), 1)
+        return jnp.where(head == t * count + lane // each, 1.0, 0.0).astype(jnp.bfloat16)
 
     def widen(array, matrix):
-        return jnp.dot(array, matrix, precision=EXACT, preferred_element_type=jnp.float32)
+        return jnp.dot(array, matrix, preferred_element_type=jnp.float32)
 
     def state_copy(t):
         return pltpu.make_async_remote_copy(
@@ -418,6 +444,7 @@
 
     lax.fori_loop(0, value_tiles, first_pass, 0)
     squares[...] = jnp.zeros_like(squares)
+    skip_parts = three_parts(jnp.broadcast_to(skip_gain[...], (16, heads)))
     left_half = lax.broadcasted_iota(jnp.int32, (BLOCK, BLOCK), 1) < TILE // width
 
     def second_pass(t, _):
@@ -442,7 +469,7 @@
         g = t // group_tiles
         columns = widen(cum_s[...], spread(t, BLOCK, width))
         place = pl.ds(pl.multiple_of(t * TILE, TILE), TILE)
-        skip = widen(jnp.broadcast_to(skip_gain[...], (8, heads)), spread(t, TILE // width, width))[0:1]
+        skip = widen(skip_parts, spread(t, TILE // width, width))[0:1]
         for b in range(blocks):
             lo = b * BLOCK
             value = acts[t, pl.ds(lo, BLOCK), :]
@@ -595,11 +622,13 @@
     slab_rows = length * n
     value_tiles, key_tiles = columns // TILE, key_cols // TILE
     tiles = 2 * value_tiles + 2 * key_tiles
+    quarters = 4
+    deep = depth // quarters
     bf16, f32 = jnp.bfloat16, jnp.float32
     vmem, anywhere = pl.BlockSpec(memory_space=pltpu.VMEM), pl.BlockSpec(memory_space=pl.ANY)
     dma = pltpu.SemaphoreType.DMA
     pre, step_raw = pl.pallas_call(
-        functools.partial(project_kernel, n, tiles),
+        functools.partial(project_kernel, n, tiles, quarters),
         out_shape=(
             jax.ShapeDtypeStruct((tiles, slab_rows, TILE), bf16),
             jax.ShapeDtypeStruct((slab_rows, heads), f32),
@@ -607,15 +636,17 @@
         in_specs=[vmem] + [anywhere] * 5,
         out_specs=(vmem, vmem),
         scratch_shapes=[
-            pltpu.VMEM((n, length, depth), bf16),
-            pltpu.VMEM((tiles, depth, TILE), bf16),
-            pltpu.VMEM((depth, heads), bf16),
-            dma((tiles,)), dma, dma((n,)), dma((n,)), dma((n,)),
+            pltpu.VMEM((quarters, slab_rows, deep), bf16),
+            pltpu.VMEM((quarters, tiles, deep, TILE), bf16),
+            pltpu.VMEM((heads, depth), bf16),
+            pltpu.VMEM((tiles, slab_rows, TILE), f32),
+            pltpu.VMEM((slab_rows, heads), f32),
+            dma((quarters, tiles)), dma, dma((quarters, n)), dma((quarters, n)), dma((quarters, n)),
         ],
         compiler_params=pltpu.CompilerParams(
             collective_id=0, has_side_effects=True, vmem_limit_bytes=56 * 2**20
         ),
-    )(tokens, gate_weight, value_weight, key_weight, query_weight, step_weight)
+    )(tokens, gate_weight, value_weight, key_weight, query_weight, step_weight.T)
     blocks = slab_rows // BLOCK
     groups_here = key_cols // STATE
     out_cols = out_weight.shape[1]
@@ -625,7 +656,7 @@
     conv_tiles = value_tiles + 2 * key_tiles
     return pl.pallas_call(
         functools.partial(layer_kernel, n, slabs, value_tiles, key_tiles),
-        out_shape=jax.ShapeDtypeStruct((length, out_cols), bf16),
+        out_shape=jax.ShapeDtypeStruct((length, out_cols), f32),
         in_specs=[vmem] * 9 + [anywhere],
         out_specs=vmem,
         scratch_shapes=[
@@ -636,11 +667,11 @@
             pltpu.VMEM((groups_here, slab_rows, STATE), bf16),
             pltpu.VMEM((groups_here, blocks, BLOCK, BLOCK), f32),
             pltpu.VMEM(wide, bf16),
-            pltpu.VMEM((slab_rows, heads), f32),
+            pltpu.VMEM((slab_rows, 3 * heads), bf16),
             pltpu.VMEM((blocks, heads, BLOCK), f32),
             pltpu.VMEM((blocks, heads, BLOCK), f32),
-            pltpu.VMEM((slab_rows, heads), f32),
-            pltpu.VMEM((slab_rows, heads), f32),
+            pltpu.VMEM((slab_rows, 3 * heads), bf16),
+            pltpu.VMEM((slab_rows, 3 * heads), bf16),
             pltpu.VMEM(wide, f32),
             pltpu.VMEM((max(blocks - 1, 1), value_tiles, STATE, TILE), f32),
             pltpu.VMEM((value_tiles, STATE, TILE), f32),
@@ -662,7 +693,7 @@
     )(
         pre, step_raw, value_conv, key_conv, query_conv, step_bias[None], decay_log[None],
         skip_gain[None], norm_gain[None], out_weight,
-    )
+    ).astype(bf16)
 
 
 def solution(mesh):

time: 127 us -> 114 us (0.90)
  Pallas kernels: 123 us -> 112 us
  local copies, waits for them, and re-layouts: 4.13 us -> 0 us
  other arithmetic: 0 us -> 2.07 us
    pallas_call x1, Pallas kernels: 70.7 us -> 60.9 us  [fused(): pl.pallas_call(functools.partial(layer_kernel, n, slabs, value_tiles, key...]
    unnamed x2 -> x0, local copies, waits for them, and re-layouts: 4.13 us -> none
    convert_element_type x0 -> x1, other arithmetic: none -> 2.07 us  [fused(): return pl.pallas_call(functools.partial(layer_kernel, n, slabs, value_til...]
    pallas_call x1, Pallas kernels: 52.3 us -> 50.9 us  [fused(): pl.pallas_call(functools.partial(project_kernel, n, tiles, quarters), out...]
where the time goes in v2:
time: 114 us
  Pallas kernels  112 us (98%)
  other arithmetic  2.07 us (2%)
    pallas_call x1, Pallas kernels, fused(): pl.pallas_call(functools.partial(layer_kernel, n, slabs, value_tiles, key...  60.9 us
    pallas_call x1, Pallas kernels, fused(): pl.pallas_call(functools.partial(project_kernel, n, tiles, quarters), out...  50.9 us

profile of v2, /device:TPU:19, one launch (start us, length us, event | category | flops | bytes accessed | tf_op | source)
XLA Modules:
  0.0 113.9 jit_solution(1759809219946142141)
XLA Ops:
  0.0 50.9 %shard_map.136 = (bf16[18,256,256]{2,1,0:T(8,128)(2,1)}, f32[256,32]{1,0:T(8,128)}) custom-call(bf16[64,4096]{1,0:T(8,128)(2,1)} %tokens.1, bf16[4096,2048]{1,0:T(8,128)(2,1)} %gate_w.1, bf16[4096,2048]{1,0:T(8,128)(2,1)} %value_w.1, bf16[4096,256]{1,0:T(8,128)(2,1)} %key_w.1, bf16[4096,256]{1,0:T(8,128)(2,1)} %query_w.1, bf16[32,4096]{1,0:T(8,128)(2,1)} %bitcast.5), custom_call_target="tpu_custom_call" | custom-call | tf_op jit(solution)/shard_map/pallas_call | solution.py:630
  50.9 60.9 %shard_map.137 = f32[64,4096]{1,0:T(8,128)} custom-call(bf16[18,256,256]{2,1,0:T(8,128)(2,1)} %get-tuple-element.7.pre, f32[256,32]{1,0:T(8,128)} %get-tuple-element.8.step_raw, f32[4,2048]{1,0:T(4,128)} %value_conv.1, f32[4,256]{1,0:T(4,128)} %key_conv.1, f32[4,256]{1,0:T(4,128)} %query_conv.1, f32[1,32]{1,0:T(1,128)} %bitcast.7, f32[1,32]{1,0:T(1,128)} %bitcast.8, ...), custom_call_target="tpu_custom_call" | custom-call | tf_op jit(solution)/shard_map/pallas_call | solution.py:657
  111.8 2.1 %convert_element_type.3 = bf16[64,4096]{1,0:T(8,128)(2,1)} convert(f32[64,4096]{1,0:T(8,128)} %shard_map.137) | non-fusion elementwise | flops 262144 | bytes 1572864 | tf_op jit(solution)/shard_map/convert_element_type | solution.py:696

commit v3 on v2

--- a/solution.py
+++ b/solution.py
@@ -195,7 +195,7 @@
             for part in range(source.shape[1] // TILE):
                 pltpu.make_async_copy(
                     source.at[pl.ds(q * deep, deep), pl.ds(part * TILE, TILE)],
-                    weights.at[q, tile], weight_sem.at[q, tile],
+                    weights.at[q, tile // 2, :, pl.ds(tile % 2 * TILE, TILE)], weight_sem.at[q, tile],
                 ).start()
                 tile += 1
 
@@ -258,20 +258,23 @@
     for q in range(quarters):
         receive(q, n - 1)
 
-        def one(t, _):
-            pltpu.make_async_copy(
-                gate_w.at[pl.ds(0, deep), pl.ds(0, TILE)], weights.at[q, t], weight_sem.at[q, t]
-            ).wait()
-            added = jnp.dot(rows[q], weights[q, t], preferred_element_type=jnp.float32)
+        def one(pair, _):
+            for half in range(2):
+                pltpu.make_async_copy(
+                    gate_w.at[pl.ds(0, deep), pl.ds(0, TILE)],
+                    weights.at[q, pair, :, pl.ds(half * TILE, TILE)], weight_sem.at[q, 2 * pair + half],
+                ).wait()
+            added = jnp.dot(rows[q], weights[q, pair], preferred_element_type=jnp.float32)
             if q > 0:
-                added = total[t] + added
+                added = total[pair] + added
             if q < quarters - 1:
-                total[t] = added
+                total[pair] = added
             else:
-                pre[t] = added.astype(jnp.bfloat16)
+                for half in range(2):
+                    pre[2 * pair + half] = added[:, half * TILE:(half + 1) * TILE].astype(jnp.bfloat16)
             return 0
 
-        lax.fori_loop(0, tiles, one, 0)
+        lax.fori_loop(0, tiles // 2, one, 0)
         added = lax.dot_general(
             rows[q], step_buf[:, q * deep:(q + 1) * deep], (((1,), (1,)), ((), ())),
             preferred_element_type=jnp.float32,
@@ -312,7 +315,7 @@
     pre, step_raw, value_conv, key_conv, query_conv, step_bias, decay_log, skip_gain, norm_gain, out_w,
     out,
     border, edge_buf, padded, keys, queries, scores, acts, cum_s, cum_t, step_t, tail_s, grow_s,
-    grow_x, local0, slab, leaving, inflow, gated, squares, normed, weight, partial, from_left, from_right,
+    grow_x, local0, slab, leaving, inflow, starts, gated, squares, normed, weight, partial, from_left, from_right,
     edge_send, edge_recv, state_send, state_recv, weight_sem, part_send, left_recv, right_recv,
 ):
     me = lax.axis_index("tp")
@@ -430,8 +433,8 @@
                 preferred_element_type=jnp.float32,
             )
             state = grow[lo + BLOCK - 1:lo + BLOCK] * state + added
-            if b < blocks - 1:
-                local0[b, t] = state
+            if b == 0:
+                local0[t] = state
         slab[t] = state
 
         @pl.when(ctx == 0)
@@ -447,7 +450,7 @@
     skip_parts = three_parts(jnp.broadcast_to(skip_gain[...], (16, heads)))
     left_half = lax.broadcasted_iota(jnp.int32, (BLOCK, BLOCK), 1) < TILE // width
 
-    def second_pass(t, _):
+    def enter(t):
         grow = grow_x[t]
 
         @pl.when(ctx > 0)
@@ -455,57 +458,56 @@
             state_copy(t).wait_recv()
 
         start = inflow[t].astype(jnp.float32)
-        fall = jnp.ones((1, TILE), jnp.float32)
-        falls = []
-        for b in range(blocks):
-            falls.append(fall)
-            fall = fall * grow[(b + 1) * BLOCK - 1:(b + 1) * BLOCK]
+        after = grow[BLOCK - 1:BLOCK] * start + local0[t]
+        starts[0, t] = inflow[t]
+        starts[1, t] = after.astype(jnp.bfloat16)
 
         @pl.when(jnp.logical_and(ctx > 0, ctx < slabs - 1))
         def _():
+            fall = grow[BLOCK - 1:BLOCK] * grow[2 * BLOCK - 1:2 * BLOCK]
             leaving[t] = (fall * start + slab[t]).astype(jnp.bfloat16)
             state_copy(t).start()
 
-        g = t // group_tiles
-        columns = widen(cum_s[...], spread(t, BLOCK, width))
-        place = pl.ds(pl.multiple_of(t * TILE, TILE), TILE)
-        skip = widen(skip_parts, spread(t, TILE // width, width))[0:1]
-        for b in range(blocks):
-            lo = b * BLOCK
-            value = acts[t, pl.ds(lo, BLOCK), :]
+    def second_pass(b, first):
+        rows_b = pl.ds(pl.multiple_of(b * BLOCK, BLOCK), BLOCK)
+
+        def one(t, _):
+            if first:
+                enter(t)
+            g = t // group_tiles
+            columns = widen(cum_s[rows_b, :], spread(t, BLOCK, width))
+            skip = widen(skip_parts, spread(t, TILE // width, width))[0:1]
+            value = acts[t, rows_b, :]
+            score = scores[g, b]
             parts = []
             for pair in range(width // 2):
                 both = []
                 for k in (2 * pair, 2 * pair + 1):
                     h = t * width + k
-                    diff = columns[lo:lo + BLOCK, k * BLOCK:(k + 1) * BLOCK] - cum_t[b, pl.ds(h, 1), :]
+                    diff = columns[:, k * BLOCK:(k + 1) * BLOCK] - cum_t[b, pl.ds(h, 1), :]
                     factor = jnp.exp(jnp.where(causal, diff, -1e30))
-                    mix = (scores[g, b] * factor * step_t[b, pl.ds(h, 1), :]).astype(jnp.bfloat16)
+                    mix = (score * factor * step_t[b, pl.ds(h, 1), :]).astype(jnp.bfloat16)
                     both.append(jnp.dot(
                         mix, value[:, pair * BLOCK:(pair + 1) * BLOCK], preferred_element_type=jnp.float32
                     ))
                 parts.append(jnp.where(left_half, both[0], both[1]))
             inner = jnp.concatenate(parts, axis=1)
-            enter = start if b == 0 else falls[b] * start + local0[b - 1, t]
-            outer = jnp.dot(
-                queries[g, pl.ds(lo, BLOCK), :], enter.astype(jnp.bfloat16), preferred_element_type=jnp.float32
-            )
-            ssm = inner + grow[lo:lo + BLOCK] * outer + skip * value.astype(jnp.float32)
-            gate = pre[t, pl.ds(lo, BLOCK), :].astype(jnp.float32)
-            result = ssm * silu(gate)
-            gated[t, pl.ds(lo, BLOCK), :] = result
-            squares[g, pl.ds(lo, BLOCK), :] += result * result
-        return 0
-
-    lax.fori_loop(0, value_tiles, second_pass, 0)
-    groups_here = value_tiles // group_tiles
-    for g in range(groups_here):
-        scale = lax.rsqrt(jnp.sum(squares[g], axis=1, keepdims=True) / (INNER // GROUPS) + 1e-05)
-        for t in range(g * group_tiles, (g + 1) * group_tiles):
-            cols = slice(t * TILE, (t + 1) * TILE)
-            normed[:, cols] = (gated[t] * scale * norm_gain[:, cols]).astype(jnp.bfloat16)
-
-    weight_copy.wait()
+            outer = jnp.dot(queries[g, rows_b, :], starts[b, t], preferred_element_type=jnp.float32)
+            ssm = inner + grow_x[t, rows_b, :] * outer + skip * value.astype(jnp.float32)
+            result = ssm * silu(pre[t, rows_b, :].astype(jnp.float32))
+            gated[t, rows_b, :] = result
+            squares[g, rows_b, :] += result * result
+            return 0
+
+        lax.fori_loop(0, value_tiles, one, 0)
+        for g in range(value_tiles // group_tiles):
+            total = jnp.sum(squares[g, rows_b, :], axis=1, keepdims=True)
+            scale = lax.rsqrt(total / (INNER // GROUPS) + 1e-05)
+            for t in range(g * group_tiles, (g + 1) * group_tiles):
+                cols = slice(t * TILE, (t + 1) * TILE)
+                normed[rows_b, cols] = (
+                    gated[t, rows_b, :] * scale * norm_gain[:, cols]
+                ).astype(jnp.bfloat16)
 
     def product(b, p):
         rows = normed[pl.ds(pl.multiple_of(b * length, length), length), :]
@@ -528,7 +530,7 @@
             device_id={"tp": me - 1}, device_id_type=MESH,
         )
 
-    for far in range(n - 1, 0, -1):
+    def send(far):
         above, below = me + far, me - far
 
         def forward(p, _):
@@ -570,6 +572,26 @@
 
         lax.fori_loop(0, pieces, forward, 0)
 
+    first_block = 1 - me // (n // 2)
+    at_end = jnp.logical_or(me == 0, me == n - 1)
+    second_pass(first_block, True)
+    weight_copy.wait()
+
+    @pl.when(at_end)
+    def _():
+        for far in range(n - 1, n // 2 - 1, -1):
+            send(far)
+
+    second_pass(1 - first_block, False)
+
+    @pl.when(jnp.logical_not(at_end))
+    def _():
+        for far in range(n - 2, n // 2 - 1, -1):
+            send(far)
+
+    for far in range(n // 2 - 1, 0, -1):
+        send(far)
+
     for p in range(pieces):
         cols = pl.ds(p * piece, piece)
         partial[me, p] = product(me, p).astype(jnp.bfloat16)
@@ -616,6 +638,11 @@
 def fused(n, slabs, tokens, gate_weight, value_weight, key_weight, query_weight, step_weight,
           value_conv, key_conv, query_conv, step_bias, decay_log, skip_gain, norm_gain, out_weight):
     length, depth = tokens.shape
+    if length * n != 2 * BLOCK or n != 4:
+        return shards(
+            tokens, gate_weight, value_weight, key_weight, query_weight, step_weight, value_conv, key_conv,
+            query_conv, step_bias, decay_log, skip_gain, norm_gain, out_weight,
+        )
     columns = gate_weight.shape[1]
     key_cols = key_weight.shape[1]
     heads = step_weight.shape[1]
@@ -637,9 +664,9 @@
         out_specs=(vmem, vmem),
         scratch_shapes=[
             pltpu.VMEM((quarters, slab_rows, deep), bf16),
-            pltpu.VMEM((quarters, tiles, deep, TILE), bf16),
+            pltpu.VMEM((quarters, tiles // 2, deep, 2 * TILE), bf16),
             pltpu.VMEM((heads, depth), bf16),
-            pltpu.VMEM((tiles, slab_rows, TILE), f32),
+            pltpu.VMEM((tiles // 2, slab_rows, 2 * TILE), f32),
             pltpu.VMEM((slab_rows, heads), f32),
             dma((quarters, tiles)), dma, dma((quarters, n)), dma((quarters, n)), dma((quarters, n)),
         ],
@@ -656,7 +683,7 @@
     conv_tiles = value_tiles + 2 * key_tiles
     return pl.pallas_call(
         functools.partial(layer_kernel, n, slabs, value_tiles, key_tiles),
-        out_shape=jax.ShapeDtypeStruct((length, out_cols), f32),
+        out_shape=jax.ShapeDtypeStruct((length, out_cols), bf16),
         in_specs=[vmem] * 9 + [anywhere],
         out_specs=vmem,
         scratch_shapes=[
@@ -673,10 +700,11 @@
             pltpu.VMEM((slab_rows, 3 * heads), bf16),
             pltpu.VMEM((slab_rows, 3 * heads), bf16),
             pltpu.VMEM(wide, f32),
-            pltpu.VMEM((max(blocks - 1, 1), value_tiles, STATE, TILE), f32),
+            pltpu.VMEM((value_tiles, STATE, TILE), f32),
             pltpu.VMEM((value_tiles, STATE, TILE), f32),
             pltpu.VMEM((value_tiles, STATE, TILE), bf16),
             pltpu.VMEM((value_tiles, STATE, TILE), bf16),
+            pltpu.VMEM((2, value_tiles, STATE, TILE), bf16),
             pltpu.VMEM(wide, f32),
             pltpu.VMEM((groups_here, slab_rows, TILE), f32),
             pltpu.VMEM((slab_rows, columns), bf16),
@@ -693,7 +721,7 @@
     )(
         pre, step_raw, value_conv, key_conv, query_conv, step_bias[None], decay_log[None],
         skip_gain[None], norm_gain[None], out_weight,
-    ).astype(bf16)
+    )
 
 
 def solution(mesh):

time: 114 us -> 107 us (0.939)
  Pallas kernels: 112 us -> 105 us
  other arithmetic: 2.07 us -> 0 us
  local copies, waits for them, and re-layouts: 0 us -> 1.87 us
    pallas_call x1, Pallas kernels: 50.9 us -> 44.7 us  [fused(): pl.pallas_call(functools.partial(project_kernel, n, tiles, quarters), out...]
    convert_element_type x1 -> x0, other arithmetic: 2.07 us -> none  [fused(): return pl.pallas_call(functools.partial(layer_kernel, n, slabs, value_til...]
    unnamed x0 -> x1, local copies, waits for them, and re-layouts: none -> 1.87 us
where the time goes in v3:
time: 107 us
  Pallas kernels  105 us (98%)
  local copies, waits for them, and re-layouts  1.87 us (2%)
    pallas_call x1, Pallas kernels, fused(): pl.pallas_call(functools.partial(layer_kernel, n, slabs, value_tiles, key...  60.6 us
    pallas_call x1, Pallas kernels, fused(): pl.pallas_call(functools.partial(project_kernel, n, tiles, quarters), out...  44.7 us

profile of v3, /device:TPU:19, one launch (start us, length us, event | category | flops | bytes accessed | tf_op | source)
XLA Modules:
  0.0 107.2 jit_solution(15887361500445786515)
XLA Ops:
  0.0 44.7 %shard_map.136 = (bf16[18,256,256]{2,1,0:T(8,128)(2,1)}, f32[256,32]{1,0:T(8,128)}) custom-call(bf16[64,4096]{1,0:T(8,128)(2,1)} %tokens.1, bf16[4096,2048]{1,0:T(8,128)(2,1)} %gate_w.1, bf16[4096,2048]{1,0:T(8,128)(2,1)} %value_w.1, bf16[4096,256]{1,0:T(8,128)(2,1)} %key_w.1, bf16[4096,256]{1,0:T(8,128)(2,1)} %query_w.1, bf16[32,4096]{1,0:T(8,128)(2,1)} %bitcast.5), custom_call_target="tpu_custom_call" | custom-call | tf_op jit(solution)/shard_map/pallas_call | solution.py:657
  44.7 60.6 %shard_map.137 = bf16[64,4096]{1,0:T(8,128)(2,1)} custom-call(bf16[18,256,256]{2,1,0:T(8,128)(2,1)} %get-tuple-element.7.pre, f32[256,32]{1,0:T(8,128)} %get-tuple-element.8.step_raw, f32[4,2048]{1,0:T(4,128)} %value_conv.1, f32[4,256]{1,0:T(4,128)} %key_conv.1, f32[4,256]{1,0:T(4,128)} %query_conv.1, f32[1,32]{1,0:T(1,128)} %bitcast.7, f32[1,32]{1,0:T(1,128)} %bitcast.8, ...), custom_call_target="tpu_custom_call" | custom-call | tf_op jit(solution)/shard_map/pallas_call | solution.py:684
  105.4 1.9 %copy.16 = bf16[64,4096]{1,0:T(8,128)(2,1)} copy(bf16[64,4096]{1,0:T(8,128)(2,1)} %shard_map.137) | data formatting | bytes 1048576

commit v4 on v3

--- a/solution.py
+++ b/solution.py
@@ -251,40 +251,48 @@
             def _():
                 leftward(q, above).start()
 
-    for far in range(1, n - 1):
-        for q in range(quarters):
-            receive(q, far)
+    def multiply(q, half, first):
+        part = pl.ds(pl.multiple_of(half * 2 * length, 2 * length), 2 * length)
+
+        def one(pair, _):
+            if first:
+                for side in range(2):
+                    pltpu.make_async_copy(
+                        gate_w.at[pl.ds(0, deep), pl.ds(0, TILE)],
+                        weights.at[q, pair, :, pl.ds(side * TILE, TILE)], weight_sem.at[q, 2 * pair + side],
+                    ).wait()
+            added = jnp.dot(rows[q, part, :], weights[q, pair], preferred_element_type=jnp.float32)
+            if q > 0:
+                added = total[pair, part, :] + added
+            if q < quarters - 1:
+                total[pair, part, :] = added
+            else:
+                for side in range(2):
+                    pre[2 * pair + side, part, :] = added[:, side * TILE:(side + 1) * TILE].astype(jnp.bfloat16)
+            return 0
+
+        lax.fori_loop(0, tiles // 2, one, 0)
+        added = lax.dot_general(
+            rows[q, part, :], step_buf[:, q * deep:(q + 1) * deep], (((1,), (1,)), ((), ())),
+            preferred_element_type=jnp.float32,
+        )
+        if q > 0:
+            added = step_total[part, :] + added
+        if q < quarters - 1:
+            step_total[part, :] = added
+        else:
+            step_raw[part, :] = added
+
+    own = me // 2
     step_copy.wait()
     for q in range(quarters):
-        receive(q, n - 1)
-
-        def one(pair, _):
-            for half in range(2):
-                pltpu.make_async_copy(
-                    gate_w.at[pl.ds(0, deep), pl.ds(0, TILE)],
-                    weights.at[q, pair, :, pl.ds(half * TILE, TILE)], weight_sem.at[q, 2 * pair + half],
-                ).wait()
-            added = jnp.dot(rows[q], weights[q, pair], preferred_element_type=jnp.float32)
-            if q > 0:
-                added = total[pair] + added
-            if q < quarters - 1:
-                total[pair] = added
-            else:
-                for half in range(2):
-                    pre[2 * pair + half] = added[:, half * TILE:(half + 1) * TILE].astype(jnp.bfloat16)
-            return 0
-
-        lax.fori_loop(0, tiles // 2, one, 0)
-        added = lax.dot_general(
-            rows[q], step_buf[:, q * deep:(q + 1) * deep], (((1,), (1,)), ((), ())),
-            preferred_element_type=jnp.float32,
-        )
-        if q > 0:
-            added = step_total[...] + added
-        if q < quarters - 1:
-            step_total[...] = added
-        else:
-            step_raw[...] = added
+        receive(q, 1)
+        multiply(q, own, True)
+    for q in range(quarters):
+        receive(q, 2)
+    for q in range(quarters):
+        receive(q, 3)
+        multiply(q, 1 - own, False)
 
     for q in range(quarters):
         for chunk in range(n):

time: 107 us -> 103 us (0.963)
  Pallas kernels: 105 us -> 101 us
    pallas_call x1, Pallas kernels: 44.7 us -> 40.7 us  [fused(): pl.pallas_call(functools.partial(project_kernel, n, tiles, quarters), out...]
where the time goes in v4:
time: 103 us
  Pallas kernels  101 us (98%)
  local copies, waits for them, and re-layouts  1.87 us (2%)
    pallas_call x1, Pallas kernels, fused(): pl.pallas_call(functools.partial(layer_kernel, n, slabs, value_tiles, key...  60.2 us
    pallas_call x1, Pallas kernels, fused(): pl.pallas_call(functools.partial(project_kernel, n, tiles, quarters), out...  40.7 us

profile of v4, /device:TPU:19, one launch (start us, length us, event | category | flops | bytes accessed | tf_op | source)
XLA Modules:
  0.0 102.8 jit_solution(16507795260357026308)
XLA Ops:
  0.0 40.7 %shard_map.136 = (bf16[18,256,256]{2,1,0:T(8,128)(2,1)}, f32[256,32]{1,0:T(8,128)}) custom-call(bf16[64,4096]{1,0:T(8,128)(2,1)} %tokens.1, bf16[4096,2048]{1,0:T(8,128)(2,1)} %gate_w.1, bf16[4096,2048]{1,0:T(8,128)(2,1)} %value_w.1, bf16[4096,256]{1,0:T(8,128)(2,1)} %key_w.1, bf16[4096,256]{1,0:T(8,128)(2,1)} %query_w.1, bf16[32,4096]{1,0:T(8,128)(2,1)} %bitcast.5), custom_call_target="tpu_custom_call" | custom-call | tf_op jit(solution)/shard_map/pallas_call | solution.py:665
  40.7 60.2 %shard_map.137 = bf16[64,4096]{1,0:T(8,128)(2,1)} custom-call(bf16[18,256,256]{2,1,0:T(8,128)(2,1)} %get-tuple-element.7.pre, f32[256,32]{1,0:T(8,128)} %get-tuple-element.8.step_raw, f32[4,2048]{1,0:T(4,128)} %value_conv.1, f32[4,256]{1,0:T(4,128)} %key_conv.1, f32[4,256]{1,0:T(4,128)} %query_conv.1, f32[1,32]{1,0:T(1,128)} %bitcast.7, f32[1,32]{1,0:T(1,128)} %bitcast.8, ...), custom_call_target="tpu_custom_call" | custom-call | tf_op jit(solution)/shard_map/pallas_call | solution.py:692
  100.9 1.9 %copy.16 = bf16[64,4096]{1,0:T(8,128)(2,1)} copy(bf16[64,4096]{1,0:T(8,128)(2,1)} %shard_map.137) | data formatting | bytes 1048576
